TPU v7x, 256 devices: a whole 4x4x8 slice. The times are simulated.
256 devices in a mesh: dp: 4 (over x), ex: 16 (over z, y_hi), ey: 4 (over y_lo, core).
Axes of the slice: x: 4, y: 4 (y_hi: 2, y_lo: 2; y = y_hi * 2 + y_lo), z: 8, core: 2. Of those that a mesh axis runs over, the one named last changes fastest.
Arguments:
- tokens: bfloat16 [2, 12288, 2048], P(None, ('dp', 'ex', 'ey')), parts along dimension 1, may hold values from -6 to 6
- expert_ids: int32 [2, 12288, 8], P(None, ('dp', 'ex', 'ey')), parts along dimension 1, may hold values from 0 to 63, as said below
- slot_ids: int32 [2, 12288, 8], P(None, ('dp', 'ex', 'ey')), parts along dimension 1, may hold values from -1 to 7, as said below
- gate_values: float32 [2, 12288, 8], P(None, ('dp', 'ex', 'ey')), parts along dimension 1, may hold values from 0.05 to 1
- gate_weight: bfloat16 [64, 2048, 1024], P(('ex', 'ey')), may hold values from -0.125 to 0.125
- up_weight: bfloat16 [64, 2048, 1024], P(('ex', 'ey')), may hold values from -0.125 to 0.125
- down_weight: bfloat16 [64, 1024, 2048], P(('ex', 'ey')), may hold values from -0.1875 to 0.1875
Outputs:
- mixture: bfloat16 [2, 12288, 2048], P(None, ('dp', 'ex', 'ey')), parts along dimension 1
There are 4 independent parts, one for each index of `dp`. A program takes and returns all parts, laid end to end along the dimension named above; an argument that names none is the same for every part. Nothing has to cross between parts.
Inputs may be any that keep to these rules, and one draw needn't show every extreme that they name: `expert_ids`: each token names 8 different experts. `slot_ids`: within one micro-batch, one block of 48 tokens and one expert, the assignments are numbered 0, 1, 2, ... in a drawn priority order; an assignment keeps its number as slot if it is below 8, else it is -1. In every block some expert receives an assignment from each of its 48 tokens.
All inputs are finite; a program needn't handle non-finite values.
Results may differ from a plain program's by a relative error of at most 0.0057.
Values may be sent and summed in bfloat16 or wider, within the bound.
A program may use at most 64 MiB of HBM per device.

v0:
```python
import jax
import jax.numpy as jnp
from jax import lax
from jax.sharding import PartitionSpec as P

TOP = 8


def per_device(tokens, expert_ids, slot_ids, gate_values, gate_weight, up_weight, down_weight):
    across_x = lax.axis_size("ex")
    across_y = lax.axis_size("ey")
    experts = across_x * across_y
    micro, tok_dev, width = tokens.shape
    slot_count = (tok_dev * TOP * 5 + 4 * experts - 1) // (4 * experts)
    cells = experts * slot_count
    gate_matrix = gate_weight[0]
    up_matrix = up_weight[0]
    down_matrix = down_weight[0]
    columns = jnp.arange(cells, dtype=jnp.int32)

    def expert_apply(received):
        flat = received.reshape(-1, width)
        gate_part = jnp.dot(flat, gate_matrix, preferred_element_type=jnp.float32)
        up_part = jnp.dot(flat, up_matrix, preferred_element_type=jnp.float32)
        hidden = (jax.nn.silu(gate_part) * up_part).astype(jnp.bfloat16)
        output = jnp.dot(hidden, down_matrix, preferred_element_type=jnp.float32).astype(
            jnp.bfloat16
        )
        return output.reshape(received.shape)

    def route_slots(buffer):
        return lax.all_to_all(
            expert_apply(
                lax.all_to_all(buffer, ("ex", "ey"), split_axis=0, concat_axis=0, tiled=True)
            ),
            ("ex", "ey"),
            split_axis=0,
            concat_axis=0,
            tiled=True,
        )

    buffers = []
    mixings = []
    for index in range(micro):
        chosen = expert_ids[index]
        places = slot_ids[index]
        cell_index = jnp.where(places >= 0, chosen * slot_count + places, -1)
        one_hot = cell_index[:, :, None] == columns[None, None, :]
        selection = jnp.sum(one_hot.astype(jnp.float32), axis=1).astype(jnp.bfloat16)
        mixing = jnp.sum(
            jnp.where(one_hot, gate_values[index][:, :, None], jnp.float32(0.0)), axis=1
        )
        gathered = jnp.dot(selection.T, tokens[index], preferred_element_type=jnp.float32)
        buffers.append(gathered.astype(jnp.bfloat16).reshape(experts, slot_count, width))
        mixings.append(mixing)
    outputs = [route_slots(buffers[index]) for index in range(micro)]
    results = []
    for index in range(micro):
        flat_out = outputs[index].reshape(cells, width).astype(jnp.float32)
        mixture = jnp.dot(mixings[index], flat_out, precision=lax.Precision.HIGHEST)
        results.append(mixture.astype(jnp.bfloat16))
    return jnp.stack(results, axis=0)


def solution(mesh):
    in_specs = (
        P(None, ("dp", "ex", "ey"), None),
        P(None, ("dp", "ex", "ey"), None),
        P(None, ("dp", "ex", "ey"), None),
        P(None, ("dp", "ex", "ey"), None),
        P(("ex", "ey"), None, None),
        P(("ex", "ey"), None, None),
        P(("ex", "ey"), None, None),
    )
    out_specs = P(None, ("dp", "ex", "ey"), None)
    return jax.shard_map(
        per_device, mesh=mesh, in_specs=in_specs, out_specs=out_specs, check_vma=False
    )
```

profile of v0, /device:TPU:6, one launch (start us, length us, event | category | flops | bytes accessed | tf_op | source)
XLA Modules:
  0.0 242.6 jit_solution(16407325815586133468)
XLA Ops:
  0.0 0.7 select_bitcast_fusion.1
  0.7 0.1 copy.14
  0.8 0.7 slice_bitcast_fusion.1
  1.5 0.1 copy.15
  1.6 0.5 convert_reduce_fusion
  2.2 3.0 %fusion.19 = bf16[64,8,2048]{2,1,0:T(8,128)(2,1)} fusion(bf16[2,48,2048]{2,1,0:T(8,128)(2,1)} %param.7, bf16[48,512]{1,0:T(8,128)(2,1)S(1)} %get-tuple-element.7), kind=kOutput, calls=%fused_computation.17 | convolution fusion | flops 101711872 | bytes 2342912 | tf_op jit(solution)/shard_map/dot_general | solution.py:53
  5.1 0.0 copy-start
  5.2 12.2 %all-to-all-start.2 = ((bf16[64,8,2048]{2,1,0:T(8,128)(2,1)}), bf16[64,8,2048]{2,1,0:T(8,128)(2,1)S(1)}, u32[]{:S(2)}, u32[]{:S(2)}) async-start(bf16[64,8,2048]{2,1,0:T(8,128)(2,1)} %fusion.19), calls=%async_computation.2 | async-start | bytes 4194304 | tf_op jit(solution)/shard_map/all_to_all | solution.py:34
  17.4 0.1 copy.12
  17.5 0.1 copy.13
  17.6 0.5 convert_reduce_fusion.1
  18.1 0.0 copy-done
  18.1 2.0 fusion.18
  20.2 48.6 %all-to-all-done.2 = bf16[64,8,2048]{2,1,0:T(8,128)(2,1)S(1)} async-done(((bf16[64,8,2048]{2,1,0:T(8,128)(2,1)}), bf16[64,8,2048]{2,1,0:T(8,128)(2,1)S(1)}, u32[]{:S(2)}, u32[]{:S(2)}) %all-to-all-start.2) | async-done | bytes 2097184 | tf_op jit(solution)/shard_map/all_to_all | solution.py:34
  68.8 5.6 %all-to-all-start = ((bf16[64,8,2048]{2,1,0:T(8,128)(2,1)}), bf16[64,8,2048]{2,1,0:T(8,128)(2,1)}, u32[]{:S(2)}, u32[]{:S(2)}) async-start(bf16[64,8,2048]{2,1,0:T(8,128)(2,1)} %fusion.18), calls=%async_computation | async-start | bytes 4194304 | tf_op jit(solution)/shard_map/all_to_all | solution.py:34
  74.4 5.9 %fusion.8 = f32[512,1024]{1,0:T(8,128)} fusion(bf16[1,2048,1024]{2,1,0:T(8,128)(2,1)} %param.11, bf16[64,8,2048]{2,1,0:T(8,128)(2,1)S(1)} %all-to-all-done.2), kind=kOutput, calls=%fused_computation.8 | convolution fusion | flops 2147483648 | bytes 8388608 | tf_op jit(solution)/shard_map/dot_general | solution.py:23
  80.2 9.9 %fusion.20 = bf16[64,8,2048]{2,1,0:T(8,128)(2,1)} fusion(bf16[1,1024,2048]{2,1,0:T(8,128)(2,1)} %param.13, f32[512,1024]{1,0:T(8,128)} %fusion.8, bf16[1,2048,1024]{2,1,0:T(8,128)(2,1)} %param.12, bf16[64,8,2048]{2,1,0:T(8,128)(2,1)S(1)} %all-to-all-done.2), kind=kOutput, calls=%fused_computation.18 | convolution fusion | flops 4299161600 | bytes 14680064 | tf_op jit(solution)/shard_map/dot_general | solution.py:26
  90.1 35.4 %all-to-all-done = bf16[64,8,2048]{2,1,0:T(8,128)(2,1)} async-done(((bf16[64,8,2048]{2,1,0:T(8,128)(2,1)}), bf16[64,8,2048]{2,1,0:T(8,128)(2,1)}, u32[]{:S(2)}, u32[]{:S(2)}) %all-to-all-start) | async-done | bytes 2097184 | tf_op jit(solution)/shard_map/all_to_all | solution.py:34
  125.6 5.5 %all-to-all-start.3 = ((bf16[64,8,2048]{2,1,0:T(8,128)(2,1)}), bf16[64,8,2048]{2,1,0:T(8,128)(2,1)S(1)}, u32[]{:S(2)}, u32[]{:S(2)}) async-start(bf16[64,8,2048]{2,1,0:T(8,128)(2,1)} %fusion.20), calls=%async_computation.3 | async-start | bytes 4194304 | tf_op jit(solution)/shard_map/all_to_all | solution.py:32
  131.1 6.5 %fusion.10 = f32[512,1024]{1,0:T(8,128)} fusion(bf16[1,2048,1024]{2,1,0:T(8,128)(2,1)} %param.11, bf16[64,8,2048]{2,1,0:T(8,128)(2,1)} %all-to-all-done), kind=kOutput, calls=%fused_computation.10 | convolution fusion | flops 2147483648 | bytes 8388608 | tf_op jit(solution)/shard_map/dot_general | solution.py:23
  137.6 10.6 %fusion.23 = bf16[64,8,2048]{2,1,0:T(8,128)(2,1)} fusion(bf16[1,1024,2048]{2,1,0:T(8,128)(2,1)} %param.13, f32[512,1024]{1,0:T(8,128)} %fusion.10, bf16[1,2048,1024]{2,1,0:T(8,128)(2,1)} %param.12, bf16[64,8,2048]{2,1,0:T(8,128)(2,1)} %all-to-all-done), kind=kOutput, calls=%fused_computation.19 | convolution fusion | flops 4299161600 | bytes 14680064 | tf_op jit(solution)/shard_map/dot_general | solution.py:26
  148.1 34.1 %all-to-all-done.3 = bf16[64,8,2048]{2,1,0:T(8,128)(2,1)S(1)} async-done(((bf16[64,8,2048]{2,1,0:T(8,128)(2,1)}), bf16[64,8,2048]{2,1,0:T(8,128)(2,1)S(1)}, u32[]{:S(2)}, u32[]{:S(2)}) %all-to-all-start.3) | async-done | bytes 2097184 | tf_op jit(solution)/shard_map/all_to_all | solution.py:32
  182.3 5.6 %all-to-all-start.1 = ((bf16[64,8,2048]{2,1,0:T(8,128)(2,1)}), bf16[64,8,2048]{2,1,0:T(8,128)(2,1)}, u32[]{:S(2)}, u32[]{:S(2)}) async-start(bf16[64,8,2048]{2,1,0:T(8,128)(2,1)} %fusion.23), calls=%async_computation.1 | async-start | bytes 4194304 | tf_op jit(solution)/shard_map/all_to_all | solution.py:32
  187.9 1.2 fusion.27
  189.1 50.0 %all-to-all-done.1 = bf16[64,8,2048]{2,1,0:T(8,128)(2,1)} async-done(((bf16[64,8,2048]{2,1,0:T(8,128)(2,1)}), bf16[64,8,2048]{2,1,0:T(8,128)(2,1)}, u32[]{:S(2)}, u32[]{:S(2)}) %all-to-all-start.1) | async-done | bytes 2097184 | tf_op jit(solution)/shard_map/all_to_all | solution.py:32
  239.1 2.8 %fusion.26 = bf16[1,48,2048]{2,1,0:T(8,128)(2,1)S(1)} fusion(f32[48,512]{1,0:T(8,128)S(1)} %get-tuple-element.6, bf16[64,8,2048]{2,1,0:T(8,128)(2,1)} %all-to-all-done.1), kind=kOutput, calls=%fused_computation.22 | convolution fusion | flops 604078080 | bytes 2392064 | tf_op jit(solution)/shard_map/dot_general | solution.py:60
  241.9 0.8 pad_maximum_fusion
Async XLA Ops:
  5.1 13.0 %copy-start = (bf16[2,48,2048]{2,1,0:T(8,128)(2,1)S(1)}, bf16[2,48,2048]{2,1,0:T(8,128)(2,1)}, u32[]{:S(2)}) copy-start(bf16[2,48,2048]{2,1,0:T(8,128)(2,1)} %param.7) | copy-start | bytes 1179652
  5.2 63.6 %all-to-all-start.2 = ((bf16[64,8,2048]{2,1,0:T(8,128)(2,1)}), bf16[64,8,2048]{2,1,0:T(8,128)(2,1)S(1)}, u32[]{:S(2)}, u32[]{:S(2)}) async-start(bf16[64,8,2048]{2,1,0:T(8,128)(2,1)} %fusion.19), calls=%async_computation.2 | async-start | bytes 4194304 | tf_op jit(solution)/shard_map/all_to_all | solution.py:34
  68.8 56.8 %all-to-all-start = ((bf16[64,8,2048]{2,1,0:T(8,128)(2,1)}), bf16[64,8,2048]{2,1,0:T(8,128)(2,1)}, u32[]{:S(2)}, u32[]{:S(2)}) async-start(bf16[64,8,2048]{2,1,0:T(8,128)(2,1)} %fusion.18), calls=%async_computation | async-start | bytes 4194304 | tf_op jit(solution)/shard_map/all_to_all | solution.py:34
  125.6 56.7 %all-to-all-start.3 = ((bf16[64,8,2048]{2,1,0:T(8,128)(2,1)}), bf16[64,8,2048]{2,1,0:T(8,128)(2,1)S(1)}, u32[]{:S(2)}, u32[]{:S(2)}) async-start(bf16[64,8,2048]{2,1,0:T(8,128)(2,1)} %fusion.20), calls=%async_computation.3 | async-start | bytes 4194304 | tf_op jit(solution)/shard_map/all_to_all | solution.py:32
  182.3 56.8 %all-to-all-start.1 = ((bf16[64,8,2048]{2,1,0:T(8,128)(2,1)}), bf16[64,8,2048]{2,1,0:T(8,128)(2,1)}, u32[]{:S(2)}, u32[]{:S(2)}) async-start(bf16[64,8,2048]{2,1,0:T(8,128)(2,1)} %fusion.23), calls=%async_computation.1 | async-start | bytes 4194304 | tf_op jit(solution)/shard_map/all_to_all | solution.py:32
where the time goes:
time: 243 us
  waiting for transfers between devices  168 us (69%)
  matrix products  41.8 us (17%)
  starting transfers between devices  29 us (12%)
  other arithmetic  2.59 us (1%)
    all_to_all x2, waiting for transfers between devices, route_slots(): lax.all_to_all(expert_apply(lax.all_to_all(buffer, ('ex', 'ey'), split_ax...  84.2 us
    all_to_all x2, waiting for transfers between devices, route_slots(): lax.all_to_all(buffer, ('ex', 'ey'), split_axis=0, concat_axis=0, tiled=T...  84 us
    dot_general x2, matrix products, expert_apply(): jnp.dot(hidden, down_matrix, preferred_element_type=jnp.float32)  20.5 us
    all_to_all x2, starting transfers between devices, route_slots(): lax.all_to_all(buffer, ('ex', 'ey'), split_axis=0, concat_axis=0, tiled=T...  17.8 us
    dot_general x2, matrix products, expert_apply(): gate_part = jnp.dot(flat, gate_matrix, preferred_element_type=jnp.float32)  12.3 us
    all_to_all x2, starting transfers between devices, route_slots(): lax.all_to_all(expert_apply(lax.all_to_all(buffer, ('ex', 'ey'), split_ax...  11.1 us
    dot_general x2, matrix products, per_device(): jnp.dot(selection.T, tokens[index], preferred_element_type=jnp.float32)  5.05 us
  transfers between devices with their start and end apart: 4, of which 4 were waited for; matrix products, arithmetic and copies ran while one was open for 15% of the time, Pallas kernels for 0%

commit v1 on v0

v1 whole, which is shorter than its diff:
```python
import functools

import jax
import jax.numpy as jnp
from jax import lax
from jax.experimental import pallas as pl
from jax.experimental.pallas import tpu as pltpu
from jax.sharding import PartitionSpec as P

MESH = pl.DeviceIdType.MESH
RING = 8
GROUP = 8
SLOTS = 8
ROWS = 2 * SLOTS
PAIR = GROUP * ROWS
PAIRS = RING // 2
UP, DOWN = 0, 1


def kernel(
    ids_ref, places_ref, gates_ref, tokens_ref, gate_ref, up_ref, down_ref, out_ref,
    wg, wu, wd, blocks, meta, turn, snd, rcv, hidden, answers, ret, acc, rs_out, rs_in, result,
    weight_sem, tok_sem, out_sem,
    meta_send, meta_recv, ag_send, ag_recv, d_send, d_recv, r_send, r_recv, rs_send, rs_recv,
):
    micro, tok, width = tokens_ref.shape
    half = width // 2
    chunks = [slice(0, half), slice(half, width)]
    ex, ey = lax.axis_index("ex"), lax.axis_index("ey")
    z = ex // 2
    me = lax.rem(ex, 2) * 4 + ey

    def along(step):
        return {"ex": lax.rem(z + step + RING, RING) * 2 + lax.rem(ex, 2), "ey": ey}

    def partner(step):
        other = lax.rem(me + step + GROUP, GROUP)
        return {"ex": z * 2 + other // 4, "ey": lax.rem(other, 4)}

    def remote(src, dst, send, recv, device):
        return pltpu.make_async_remote_copy(
            src_ref=src, dst_ref=dst, send_sem=send, recv_sem=recv,
            device_id=device, device_id_type=MESH,
        )

    tok_copies = [
        pltpu.make_async_copy(tokens_ref.at[m], blocks.at[m, 0, pl.ds(0, tok)], tok_sem.at[m])
        for m in range(micro)
    ]
    for copy in tok_copies:
        copy.start()
    weight_copies = [
        pltpu.make_async_copy(src.at[0], dst, weight_sem.at[i])
        for i, (src, dst) in enumerate(((gate_ref, wg), (up_ref, wu), (down_ref, wd)))
    ]
    for copy in weight_copies:
        copy.start()

    barrier = pltpu.get_barrier_semaphore()
    for device in [along(1), along(-1)] + [partner(r) for r in range(1, GROUP)]:
        pl.semaphore_signal(barrier, inc=1, device_id=device, device_id_type=MESH)

    turn[...] = jnp.zeros_like(turn)
    for m in range(micro):
        code = jnp.where(places_ref[m] >= 0, ids_ref[m] * SLOTS + places_ref[m], -1)
        turn[0, 0:tok, 0:8] = code.astype(jnp.float32)
        turn[1, 0:tok, 0:8] = gates_ref[m]
        meta[0, 0, m, 0:8, :] = turn[0].T[0:8]
        meta[0, 0, m, 8:16, :] = turn[1].T[0:8]

    pl.semaphore_wait(barrier, GROUP + 1)

    sent = []

    def block(m, d, way, c):
        pair, part = (d, way) if 0 < d < PAIRS else ((0, 0) if d == 0 else (0, 1))
        return blocks.at[m, pair, pl.ds(part * tok, tok), chunks[c]]

    def pass_block(m, d, way, c):
        if d == PAIRS - 1 and c != way:
            return
        copy = remote(
            block(m, d, way, c), block(m, d + 1, way, c),
            ag_send.at[m, way, d, c], ag_recv.at[m, way, d, c], along(1 if way == UP else -1),
        )
        copy.start()
        sent.append(copy)

    def await_block(m, d, way, c):
        if d == PAIRS and c != way:
            return
        remote(
            block(m, d - 1, way, c), block(m, d, way, c),
            ag_send.at[m, way, d - 1, c], ag_recv.at[m, way, d - 1, c], along(0),
        ).wait_recv()

    def meta_at(d, way):
        pair, part = (d, way) if 0 < d < PAIRS else ((0, 0) if d == 0 else (0, 1))
        return meta.at[pair, part]

    def pass_meta(d, way):
        if d == PAIRS - 1 and way != UP:
            return
        copy = remote(
            meta_at(d, way), meta_at(d + 1, way), meta_send.at[way, d], meta_recv.at[way, d],
            along(1 if way == UP else -1),
        )
        copy.start()
        sent.append(copy)

    def await_meta(d, way):
        if d == PAIRS and way != UP:
            return
        remote(
            meta_at(d - 1, way), meta_at(d, way), meta_send.at[way, d - 1], meta_recv.at[way, d - 1], along(0)
        ).wait_recv()

    lane = lax.broadcasted_iota(jnp.int32, (8, 128), 1)
    row = lax.broadcasted_iota(jnp.int32, (PAIR, 128), 0)

    def cells(m, pair):
        places = []
        for part in range(2):
            code = meta[pair, part, m, 0:8, :].astype(jnp.int32)
            expert = code // SLOTS - z * GROUP
            turned = lax.rem(expert - me + GROUP, GROUP)
            place = turned * ROWS + part * SLOTS + lax.rem(code, SLOTS)
            good = (code >= 0) & (expert >= 0) & (expert < GROUP) & (lane < tok)
            places.append(jnp.where(good, place, -1))
        return jnp.where(lane < tok, places[0], pltpu.roll(places[1], tok, 1))

    def select(m, pair):
        where = cells(m, pair)
        hit = row == where[0:1, :]
        for k in range(1, 8):
            hit = hit | (row == where[k : k + 1, :])
        return jnp.where(hit, 1.0, 0.0).astype(jnp.bfloat16)[:, 0 : 2 * tok]

    def mixing(m, pair):
        where = cells(m, pair)
        first, second = meta[pair, 0, m, 8:16, :], meta[pair, 1, m, 8:16, :]
        gates = jnp.where(lane < tok, first, pltpu.roll(second, tok, 1))
        total = jnp.zeros((PAIR, 128), jnp.float32)
        for k in range(8):
            total = total + jnp.where(row == where[k : k + 1, :], gates[k : k + 1, :], 0.0)
        total = total.T[0 : 2 * tok]
        high = total.astype(jnp.bfloat16)
        low = (total - high.astype(jnp.float32)).astype(jnp.bfloat16)
        return high, low

    def spread(m, pair, c, source, target, send, recv, back):
        for r in range(1, GROUP):
            at = pl.ds(pair * PAIR + r * ROWS, ROWS)
            copy = remote(
                source.at[m, at, chunks[c]], target.at[m, at, chunks[c]],
                send.at[m, pair, c], recv.at[m, pair, c], partner(-r if back else r),
            )
            copy.start()

    def others(buffer, m, pair, c):
        return buffer.at[m, pl.ds(pair * PAIR + ROWS, PAIR - ROWS), chunks[c]]

    def await_spread(m, pair, c, source, target, send, recv):
        remote(
            others(source, m, pair, c), others(target, m, pair, c),
            send.at[m, pair, c], recv.at[m, pair, c], along(0),
        ).wait_recv()

    def finish_spread(m, pair, c, source, target, send, recv):
        remote(
            others(source, m, pair, c), others(target, m, pair, c),
            send.at[m, pair, c], recv.at[m, pair, c], along(0),
        ).wait_send()

    def start_ring(m):
        tok_copies[m].wait()
        for c in range(2):
            for way in (UP, DOWN):
                pass_block(m, 0, way, c)

    order = [1, 2, 3, 0]
    start_ring(0)
    pass_meta(0, UP)
    pass_meta(0, DOWN)
    for m in range(micro):
        for pair in order:
            d = pair if pair else PAIRS
            for c in range(2):
                if m == 0 and c == 0:
                    for way in (UP, DOWN):
                        await_meta(d, way)
                        if d < PAIRS:
                            pass_meta(d, way)
                for way in (UP, DOWN):
                    await_block(m, d, way, c)
                    if d < PAIRS:
                        pass_block(m, d, way, c)
                if pair == 3 and c == 1 and m + 1 < micro:
                    start_ring(m + 1)
                chosen = jnp.dot(
                    select(m, pair), blocks[m, pair, :, chunks[c]], preferred_element_type=jnp.float32
                ).astype(jnp.bfloat16)
                base = pair * PAIR
                rcv[m, base : base + ROWS, chunks[c]] = chosen[0:ROWS]
                snd[m, base + ROWS : base + PAIR, chunks[c]] = chosen[ROWS:PAIR]
                spread(m, pair, c, snd, rcv, d_send, d_recv, False)

    tile = 256

    def expert(m):
        for pair in order:
            for c in range(2):
                await_spread(m, pair, c, snd, rcv, d_send, d_recv)

        @pl.loop(0, wg.shape[1] // tile)
        def _(i):
            at = pl.ds(pl.multiple_of(i * tile, tile), tile)
            gate_part = jnp.dot(rcv[m], wg[:, at], preferred_element_type=jnp.float32)
            up_part = jnp.dot(rcv[m], wu[:, at], preferred_element_type=jnp.float32)
            hidden[:, at] = (gate_part / (1.0 + jnp.exp(-gate_part)) * up_part).astype(jnp.bfloat16)

        @pl.loop(0, width // tile)
        def _(i):
            at = pl.ds(pl.multiple_of(i * tile, tile), tile)
            answer = jnp.dot(hidden[...], wd[:, at], preferred_element_type=jnp.float32)
            answers[m, :, at] = answer.astype(jnp.bfloat16)

        for pair in (0, 3, 2, 1):
            base = pair * PAIR
            for c in range(2):
                spread(m, pair, c, answers, ret, r_send, r_recv, True)
            ret[m, base : base + ROWS, :] = answers[m, base : base + ROWS, :]

    for copy in weight_copies:
        copy.wait()
    for m in range(micro):
        expert(m)

    def sum_copy(m, d, way, c):
        return remote(
            rs_out.at[m, way, d - 1, :, chunks[c]], rs_in.at[m, way, d - 1, :, chunks[c]],
            rs_send.at[m, way, d - 1, c], rs_recv.at[m, way, d - 1, c], along(-1 if way == UP else 1),
        )

    out_copies = []
    for m in range(micro):
        for pair in (0, 3, 2, 1):
            high, low = mixing(m, pair)
            base = pair * PAIR
            for c in range(2):
                await_spread(m, pair, c, answers, ret, r_send, r_recv)
                rows = ret[m, base : base + PAIR, chunks[c]]
                part = jnp.dot(high, rows, preferred_element_type=jnp.float32)
                part = part + jnp.dot(low, rows, preferred_element_type=jnp.float32)
                if pair == 0:
                    acc[m, :, chunks[c]] = part[0:tok]
                    rs_out[m, c, PAIRS - 1, :, chunks[c]] = part[tok : 2 * tok].astype(jnp.bfloat16)
                    copy = sum_copy(m, PAIRS, c, c)
                    copy.start()
                    sent.append(copy)
                    continue
                for way in (UP, DOWN):
                    mine = part[way * tok : (way + 1) * tok]
                    if pair < 3 or c == way:
                        sum_copy(m, pair + 1, way, c).wait_recv()
                        mine = mine + rs_in[m, way, pair, :, chunks[c]].astype(jnp.float32)
                    rs_out[m, way, pair - 1, :, chunks[c]] = mine.astype(jnp.bfloat16)
                    copy = sum_copy(m, pair, way, c)
                    copy.start()
                    sent.append(copy)
        for c in range(2):
            total = acc[m, :, chunks[c]]
            for way in (UP, DOWN):
                sum_copy(m, 1, way, c).wait_recv()
                total = total + rs_in[m, way, 0, :, chunks[c]].astype(jnp.float32)
            result[m, :, chunks[c]] = total.astype(jnp.bfloat16)
        copy = pltpu.make_async_copy(result.at[m], out_ref.at[m], out_sem.at[m])
        copy.start()
        out_copies.append(copy)

    for copy in sent:
        copy.wait_send()
    for m in range(micro):
        for pair in range(PAIRS):
            for c in range(2):
                finish_spread(m, pair, c, snd, rcv, d_send, d_recv)
                finish_spread(m, pair, c, answers, ret, r_send, r_recv)
    for copy in out_copies:
        copy.wait()


def per_device(tokens, expert_ids, slot_ids, gate_values, gate_weight, up_weight, down_weight):
    micro, tok, width = tokens.shape
    hid = gate_weight.shape[2]
    bf16, f32 = jnp.bfloat16, jnp.float32
    vmem = pl.BlockSpec(memory_space=pltpu.VMEM)
    anywhere = pl.BlockSpec(memory_space=pl.ANY)
    dma = pltpu.SemaphoreType.DMA
    slots = PAIRS * PAIR
    return pl.pallas_call(
        kernel,
        out_shape=jax.ShapeDtypeStruct((micro, tok, width), bf16),
        in_specs=[vmem] * 3 + [anywhere] * 4,
        out_specs=anywhere,
        scratch_shapes=[
            pltpu.VMEM((width, hid), bf16),
            pltpu.VMEM((width, hid), bf16),
            pltpu.VMEM((hid, width), bf16),
            pltpu.VMEM((micro, PAIRS, 2 * tok, width), bf16),
            pltpu.VMEM((PAIRS, 2, micro, 16, 128), f32),
            pltpu.VMEM((2, 128, 128), f32),
            pltpu.VMEM((micro, slots, width), bf16),
            pltpu.VMEM((micro, slots, width), bf16),
            pltpu.VMEM((slots, hid), bf16),
            pltpu.VMEM((micro, slots, width), bf16),
            pltpu.VMEM((micro, slots, width), bf16),
            pltpu.VMEM((micro, tok, width), f32),
            pltpu.VMEM((micro, 2, PAIRS, tok, width), bf16),
            pltpu.VMEM((micro, 2, PAIRS, tok, width), bf16),
            pltpu.VMEM((micro, tok, width), bf16),
            dma((3,)),
            dma((micro,)),
            dma((micro,)),
            dma((2, PAIRS)),
            dma((2, PAIRS)),
            dma((micro, 2, PAIRS, 2)),
            dma((micro, 2, PAIRS, 2)),
            dma((micro, PAIRS, 2)),
            dma((micro, PAIRS, 2)),
            dma((micro, PAIRS, 2)),
            dma((micro, PAIRS, 2)),
            dma((micro, 2, PAIRS, 2)),
            dma((micro, 2, PAIRS, 2)),
        ],
        compiler_params=pltpu.CompilerParams(
            collective_id=0, has_side_effects=True, vmem_limit_bytes=60 * 1024 * 1024
        ),
        cost_estimate=pl.CostEstimate(
            flops=2 * micro * slots * 3 * width * hid,
            bytes_accessed=3 * width * hid * 2,
            transcendentals=micro * slots * hid,
        ),
        name="experts",
    )(expert_ids, slot_ids, gate_values, tokens, gate_weight, up_weight, down_weight)


def solution(mesh):
    tokens = P(None, ("dp", "ex", "ey"), None)
    weights = P(("ex", "ey"), None, None)
    return jax.shard_map(
        per_device,
        mesh=mesh,
        in_specs=(tokens,) * 4 + (weights,) * 3,
        out_specs=tokens,
        check_vma=False,
    )
```

time: 243 us -> 124 us (0.51)
  waiting for transfers between devices: 168 us -> 0 us
  Pallas kernels: 0 us -> 117 us
  matrix products: 41.8 us -> 0 us
  starting transfers between devices: 29 us -> 0 us
  local copies, waits for them, and re-layouts: 1.03 us -> 5.98 us
  other arithmetic: 2.59 us -> 0 us
    all_to_all x4 -> x0, waiting for transfers between devices: 168 us -> none  [the longest x2 84.2 us: route_slots(): lax.all_to_all(expert_apply(lax.all_to_all(buffer, ('ex', 'ey'), split_ax...]
    pallas_call x0 -> x1, Pallas kernels: none -> 117 us  [per_device(): pl.pallas_call(kernel, out_shape=jax.ShapeDtypeStruct((micro, tok, width)...]
    dot_general x8 -> x0, matrix products: 41.8 us -> none  [the longest x2 20.5 us: expert_apply(): jnp.dot(hidden, down_matrix, preferred_element_type=jnp.float32)]
    all_to_all x4 -> x0, starting transfers between devices: 29 us -> none  [the longest x2 17.8 us: route_slots(): lax.all_to_all(buffer, ('ex', 'ey'), split_axis=0, concat_axis=0, tiled=T...]
    unnamed x2 -> x4, local copies, waits for them, and re-layouts: 0.01 us -> 5.98 us
  transfers between devices with their start and end apart: 4 -> 0, of which waited for: 4 -> 0; matrix products, arithmetic and copies ran while one was open for 15% -> 0% of each run, Pallas kernels for 0% -> 0%
where the time goes in v1:
time: 124 us; the launch traced here: 123 us
  Pallas kernels  117 us (94%)
  local copies, waits for them, and re-layouts  5.98 us (5%)
    pallas_call x1, Pallas kernels, per_device(): pl.pallas_call(kernel, out_shape=jax.ShapeDtypeStruct((micro, tok, width)...  117 us
    unnamed x4, local copies, waits for them, and re-layouts  5.98 us

profile of v1, /device:TPU:6, one launch (start us, length us, event | category | flops | bytes accessed | tf_op | source)
XLA Modules:
  0.0 123.2 jit_solution(17022094804100293918)
XLA Ops:
  0.0 1.4 %copy.8.ids_ref = s32[2,48,8]{2,1,0:T(8,128)} copy(s32[2,48,8]{1,2,0:T(8,128)} %param.8) | data formatting | bytes 6144 | tf_op args[1]
  1.4 1.4 %copy.9.places_ref = s32[2,48,8]{2,1,0:T(8,128)} copy(s32[2,48,8]{1,2,0:T(8,128)} %param.9) | data formatting | bytes 6144 | tf_op args[2]
  2.8 1.4 %copy.10.gates_ref = f32[2,48,8]{2,1,0:T(8,128)} copy(f32[2,48,8]{1,2,0:T(8,128)} %param.10) | data formatting | bytes 6144 | tf_op args[3]
  4.2 117.3 %experts.1 = bf16[2,48,2048]{2,1,0:T(8,128)(2,1)} custom-call(s32[2,48,8]{2,1,0:T(8,128)} %copy.8.ids_ref, s32[2,48,8]{2,1,0:T(8,128)} %copy.9.places_ref, f32[2,48,8]{2,1,0:T(8,128)} %copy.10.gates_ref, bf16[2,48,2048]{2,1,0:T(8,128)(2,1)} %tokens_ref.1, bf16[1,2048,1024]{2,1,0:T(8,128)(2,1)} %gate_ref.1, bf16[1,2048,1024]{2,1,0:T(8,128)(2,1)} %up_ref.1, ...), custom_call_target="tpu_custom_call" | custom-call | flops 12884901888 | bytes 12582912 | tf_op jit(solution)/shard_map/experts/pallas_call | solution.py:300
  121.5 1.8 %copy.12 = bf16[2,48,2048]{2,1,0:T(8,128)(2,1)} copy(bf16[2,48,2048]{2,1,0:T(8,128)(2,1)} %experts.1) | data formatting | bytes 786432

commit v2 on v0

v2 whole, which is shorter than its diff:
```python
import jax
import jax.numpy as jnp
from jax import lax
from jax.experimental import pallas as pl
from jax.experimental.pallas import tpu as pltpu
from jax.sharding import PartitionSpec as P

MESH = pl.DeviceIdType.MESH
RING = 8
FAR = RING // 2
GROUP = 8
SLOTS = 8
ROWS = 2 * SLOTS
STAGE = GROUP * ROWS
UP, DOWN = 0, 1

STAGES = 8
FIRST = 5
EARLY = (3,)
LATE = (7, 5, 6, 4, 1, 2, 0)


def place_of(m, d, way):
    if d == 0:
        return 0, m
    if d == FAR:
        return STAGES - 1, m
    return 2 * d - 1 + m, way


def kernel(
    ids_ref, places_ref, gates_ref, tokens_ref, gate_ref, up_ref, down_ref, out_ref,
    wg, wu, wd, ids, places, gates, blocks, meta, snd, rcv, hidden, answers, ret, rs_out, rs_in, result,
    weight_sem, tok_sem, route_sem, out_sem,
    meta_send, meta_recv, ag_send, ag_recv, d_send, d_recv, r_send, r_recv, rs_send, rs_recv,
):
    micro, tok, width = tokens_ref.shape
    half = width // 2
    chunks = [slice(0, half), slice(half, width)]
    ex, ey = lax.axis_index("ex"), lax.axis_index("ey")
    z = ex // 2
    me = lax.rem(ex, 2) * 4 + ey

    def along(step):
        return {"ex": lax.rem(z + step + RING, RING) * 2 + lax.rem(ex, 2), "ey": ey}

    def partner(step):
        other = lax.rem(me + step + GROUP, GROUP)
        return {"ex": z * 2 + other // 4, "ey": lax.rem(other, 4)}

    def remote(src, dst, send, recv, device):
        return pltpu.make_async_remote_copy(
            src_ref=src, dst_ref=dst, send_sem=send, recv_sem=recv,
            device_id=device, device_id_type=MESH,
        )

    barrier = pltpu.get_barrier_semaphore()
    for device in [along(1), along(-1)] + [partner(r) for r in range(1, GROUP)]:
        pl.semaphore_signal(barrier, inc=1, device_id=device, device_id_type=MESH)

    tok_copies = [
        pltpu.make_async_copy(tokens_ref.at[m], blocks.at[0, pl.ds(m * tok, tok)], tok_sem.at[m])
        for m in range(micro)
    ]
    route_copies = [
        pltpu.make_async_copy(src, dst, route_sem.at[i])
        for i, (src, dst) in enumerate(((ids_ref, ids), (places_ref, places), (gates_ref, gates)))
    ]
    weight_copies = [
        pltpu.make_async_copy(src.at[0], dst, weight_sem.at[i])
        for i, (src, dst) in enumerate(((gate_ref, wg), (up_ref, wu), (down_ref, wd)))
    ]
    for copy in tok_copies + route_copies + weight_copies:
        copy.start()

    meta[0] = jnp.zeros_like(meta[0])
    for copy in route_copies:
        copy.wait()
    for m in range(micro):
        code = jnp.where(places[m] >= 0, ids[m] * SLOTS + places[m], -1)
        meta[0, m, 0:8, 0:tok] = code.astype(jnp.float32)
        meta[0, m, 8:16, 0:tok] = gates[m]
    for copy in tok_copies:
        copy.wait()
    pl.semaphore_wait(barrier, GROUP + 1)

    sent = []

    def block(m, d, way, c):
        stage, part = place_of(m, d, way)
        return blocks.at[stage, pl.ds(part * tok, tok), chunks[c]]

    def block_copy(m, d, way, c):
        return remote(
            block(m, d, way, c), block(m, d + 1, way, c),
            ag_send.at[m, way, d, c], ag_recv.at[m, way, d, c], along(1 if way == UP else -1),
        )

    def meta_copy(m, d, way):
        return remote(
            meta.at[place_of(m, d, way)], meta.at[place_of(m, d + 1, way)],
            meta_send.at[m, way, d], meta_recv.at[m, way, d], along(1 if way == UP else -1),
        )

    def pass_block(m, d, way, c):
        if d < FAR - 1 or c == way:
            copy = block_copy(m, d, way, c)
            copy.start()
            sent.append(copy)

    def pass_meta(m, d, way):
        if d < FAR - 1 or way == UP:
            copy = meta_copy(m, d, way)
            copy.start()
            sent.append(copy)

    lane = lax.broadcasted_iota(jnp.int32, (8, 128), 1)
    row = lax.broadcasted_iota(jnp.int32, (STAGE, 128), 0)

    def cells(stage):
        found = []
        for part in range(2):
            code = meta[stage, part, 0:8, :].astype(jnp.int32)
            expert = code // SLOTS - z * GROUP
            turned = lax.rem(expert - me + GROUP, GROUP)
            place = turned * ROWS + part * SLOTS + lax.rem(code, SLOTS)
            good = (code >= 0) & (expert >= 0) & (expert < GROUP) & (lane < tok)
            found.append(jnp.where(good, place, -1))
        return jnp.where(lane < tok, found[0], pltpu.roll(found[1], tok, 1))

    def select(stage):
        where = cells(stage)
        hit = row == where[0:1, :]
        for k in range(1, 8):
            hit = hit | (row == where[k : k + 1, :])
        return jnp.where(hit, 1.0, 0.0).astype(jnp.bfloat16)[:, 0 : 2 * tok]

    def mixing(stage):
        where = cells(stage)
        first, second = meta[stage, 0, 8:16, :], meta[stage, 1, 8:16, :]
        weight = jnp.where(lane < tok, first, pltpu.roll(second, tok, 1))
        total = jnp.zeros((STAGE, 128), jnp.float32)
        for k in range(8):
            total = total + jnp.where(row == where[k : k + 1, :], weight[k : k + 1, :], 0.0)
        total = total.T[0 : 2 * tok]
        high = total.astype(jnp.bfloat16)
        low = (total - high.astype(jnp.float32)).astype(jnp.bfloat16)
        return high, low

    def spread(stage, c, source, target, send, recv, back):
        for r in range(1, GROUP):
            at = pl.ds(stage * STAGE + r * ROWS, ROWS)
            remote(
                source.at[at, chunks[c]], target.at[at, chunks[c]],
                send.at[stage, c], recv.at[stage, c], partner(-r if back else r),
            ).start()

    def whole_spread(stage, c, source, target, send, recv):
        at = pl.ds(stage * STAGE + ROWS, STAGE - ROWS)
        return remote(
            source.at[at, chunks[c]], target.at[at, chunks[c]], send.at[stage, c], recv.at[stage, c], along(0)
        )

    for m in range(micro):
        for c in range(2):
            for way in (UP, DOWN):
                pass_block(m, 0, way, c)
                if c == 0:
                    pass_meta(m, 0, way)
    for stage in range(STAGES):
        for c in range(2):
            if 0 < stage < STAGES - 1:
                d, m = (stage + 1) // 2, (stage + 1) % 2
                for way in (UP, DOWN):
                    block_copy(m, d - 1, way, c).wait_recv()
                    pass_block(m, d, way, c)
                    if c == 0:
                        meta_copy(m, d - 1, way).wait_recv()
                        pass_meta(m, d, way)
            elif stage:
                for m in range(micro):
                    block_copy(m, FAR - 1, c, c).wait_recv()
                    if c == 0:
                        meta_copy(m, FAR - 1, UP).wait_recv()
            if c == 0:
                choice = select(stage)
            chosen = jnp.dot(
                choice, blocks[stage, :, chunks[c]], preferred_element_type=jnp.float32
            ).astype(jnp.bfloat16)
            base = stage * STAGE
            rcv[base : base + ROWS, chunks[c]] = chosen[0:ROWS]
            snd[base + ROWS : base + STAGE, chunks[c]] = chosen[ROWS:STAGE]
            spread(stage, c, snd, rcv, d_send, d_recv, False)

    tile = 256

    def expert(first, last):
        at_rows = slice(first * STAGE, last * STAGE)
        for stage in range(first, last):
            for c in range(2):
                whole_spread(stage, c, snd, rcv, d_send, d_recv).wait_recv()

        @pl.loop(0, wg.shape[1] // tile)
        def _(i):
            at = pl.ds(pl.multiple_of(i * tile, tile), tile)
            gate_part = jnp.dot(rcv[at_rows], wg[:, at], preferred_element_type=jnp.float32)
            up_part = jnp.dot(rcv[at_rows], wu[:, at], preferred_element_type=jnp.float32)
            hidden[at_rows, at] = (gate_part / (1.0 + jnp.exp(-gate_part)) * up_part).astype(jnp.bfloat16)

        @pl.loop(0, width // tile)
        def _(i):
            at = pl.ds(pl.multiple_of(i * tile, tile), tile)
            answer = jnp.dot(hidden[at_rows], wd[:, at], preferred_element_type=jnp.float32)
            answers[at_rows, at] = answer.astype(jnp.bfloat16)

    def give_back(stage):
        base = stage * STAGE
        for c in range(2):
            spread(stage, c, answers, ret, r_send, r_recv, True)
        ret[base : base + ROWS, :] = answers[base : base + ROWS, :]

    for copy in weight_copies:
        copy.wait()
    expert(0, FIRST)
    for stage in EARLY:
        give_back(stage)
    expert(FIRST, STAGES)
    for stage in LATE:
        give_back(stage)

    def sum_copy(m, d, way, c):
        return remote(
            rs_out.at[m, way, d - 1, :, chunks[c]], rs_in.at[m, way, d - 1, :, chunks[c]],
            rs_send.at[m, way, d - 1, c], rs_recv.at[m, way, d - 1, c], along(-1 if way == UP else 1),
        )

    def send_sum(m, d, way, c, value):
        rs_out[m, way, d - 1, :, chunks[c]] = value.astype(jnp.bfloat16)
        copy = sum_copy(m, d, way, c)
        copy.start()
        sent.append(copy)

    for stage in reversed(range(STAGES)):
        high, low = mixing(stage)
        base = stage * STAGE
        for c in range(2):
            whole_spread(stage, c, answers, ret, r_send, r_recv).wait_recv()
            rows = ret[base : base + STAGE, chunks[c]]
            part = jnp.dot(high, rows, preferred_element_type=jnp.float32)
            part = part + jnp.dot(low, rows, preferred_element_type=jnp.float32)
            for j in range(2):
                mine = part[j * tok : (j + 1) * tok]
                if stage == STAGES - 1:
                    send_sum(j, FAR, c, c, mine)
                elif stage:
                    d, m = (stage + 1) // 2, (stage + 1) % 2
                    if d < FAR - 1 or c == j:
                        sum_copy(m, d + 1, j, c).wait_recv()
                        mine = mine + rs_in[m, j, d, :, chunks[c]].astype(jnp.float32)
                    send_sum(m, d, j, c, mine)
                else:
                    for way in (UP, DOWN):
                        sum_copy(j, 1, way, c).wait_recv()
                        mine = mine + rs_in[j, way, 0, :, chunks[c]].astype(jnp.float32)
                    result[j, :, chunks[c]] = mine.astype(jnp.bfloat16)
    out_copy = pltpu.make_async_copy(result, out_ref, out_sem)
    out_copy.start()

    for copy in sent:
        copy.wait_send()
    for stage in range(STAGES):
        for c in range(2):
            whole_spread(stage, c, snd, rcv, d_send, d_recv).wait_send()
            whole_spread(stage, c, answers, ret, r_send, r_recv).wait_send()
    out_copy.wait()


def per_device(tokens, expert_ids, slot_ids, gate_values, gate_weight, up_weight, down_weight):
    micro, tok, width = tokens.shape
    hid = gate_weight.shape[2]
    bf16, f32, i32 = jnp.bfloat16, jnp.float32, jnp.int32
    anywhere = pl.BlockSpec(memory_space=pl.ANY)
    dma = pltpu.SemaphoreType.DMA
    slots = STAGES * STAGE
    routes = [a.swapaxes(1, 2) for a in (expert_ids, slot_ids, gate_values)]
    return pl.pallas_call(
        kernel,
        out_shape=jax.ShapeDtypeStruct((micro, tok, width), bf16),
        in_specs=[anywhere] * 7,
        out_specs=anywhere,
        scratch_shapes=[
            pltpu.VMEM((width, hid), bf16),
            pltpu.VMEM((width, hid), bf16),
            pltpu.VMEM((hid, width), bf16),
            pltpu.VMEM((micro, 8, tok), i32),
            pltpu.VMEM((micro, 8, tok), i32),
            pltpu.VMEM((micro, 8, tok), f32),
            pltpu.VMEM((STAGES, 2 * tok, width), bf16),
            pltpu.VMEM((STAGES, 2, 16, 128), f32),
            pltpu.VMEM((slots, width), bf16),
            pltpu.VMEM((slots, width), bf16),
            pltpu.VMEM((slots, hid), bf16),
            pltpu.VMEM((slots, width), bf16),
            pltpu.VMEM((slots, width), bf16),
            pltpu.VMEM((micro, 2, FAR, tok, width), bf16),
            pltpu.VMEM((micro, 2, FAR, tok, width), bf16),
            pltpu.VMEM((micro, tok, width), bf16),
            dma((3,)),
            dma((micro,)),
            dma((3,)),
            dma,
            dma((micro, 2, FAR)),
            dma((micro, 2, FAR)),
            dma((micro, 2, FAR, 2)),
            dma((micro, 2, FAR, 2)),
            dma((STAGES, 2)),
            dma((STAGES, 2)),
            dma((STAGES, 2)),
            dma((STAGES, 2)),
            dma((micro, 2, FAR, 2)),
            dma((micro, 2, FAR, 2)),
        ],
        compiler_params=pltpu.CompilerParams(
            collective_id=0, has_side_effects=True, vmem_limit_bytes=60 * 1024 * 1024
        ),
        cost_estimate=pl.CostEstimate(
            flops=2 * slots * 3 * width * hid,
            bytes_accessed=3 * width * hid * 2,
            transcendentals=slots * hid,
        ),
        name="experts",
    )(*routes, tokens, gate_weight, up_weight, down_weight)


def solution(mesh):
    tokens = P(None, ("dp", "ex", "ey"), None)
    weights = P(("ex", "ey"), None, None)
    return jax.shard_map(
        per_device,
        mesh=mesh,
        in_specs=(tokens,) * 4 + (weights,) * 3,
        out_specs=tokens,
        check_vma=False,
    )
```

time: 243 us -> 114 us (0.47)
  waiting for transfers between devices: 168 us -> 0 us
  Pallas kernels: 0 us -> 111 us
  matrix products: 41.8 us -> 0 us
  starting transfers between devices: 29 us -> 0 us
  other arithmetic: 2.59 us -> 0 us
    all_to_all x4 -> x0, waiting for transfers between devices: 168 us -> none  [the longest x2 84.2 us: route_slots(): lax.all_to_all(expert_apply(lax.all_to_all(buffer, ('ex', 'ey'), split_ax...]
    pallas_call x0 -> x1, Pallas kernels: none -> 111 us  [per_device(): pl.pallas_call(kernel, out_shape=jax.ShapeDtypeStruct((micro, tok, width)...]
    dot_general x8 -> x0, matrix products: 41.8 us -> none  [the longest x2 20.5 us: expert_apply(): jnp.dot(hidden, down_matrix, preferred_element_type=jnp.float32)]
    all_to_all x4 -> x0, starting transfers between devices: 29 us -> none  [the longest x2 17.8 us: route_slots(): lax.all_to_all(buffer, ('ex', 'ey'), split_axis=0, concat_axis=0, tiled=T...]
  transfers between devices with their start and end apart: 4 -> 0, of which waited for: 4 -> 0; matrix products, arithmetic and copies ran while one was open for 15% -> 0% of each run, Pallas kernels for 0% -> 0%
where the time goes in v2:
time: 114 us; the launch traced here: 113 us
  Pallas kernels  111 us (97%)
  local copies, waits for them, and re-layouts  1.77 us (2%)
    pallas_call x1, Pallas kernels, per_device(): pl.pallas_call(kernel, out_shape=jax.ShapeDtypeStruct((micro, tok, width)...  111 us

profile of v2, /device:TPU:6, one launch (start us, length us, event | category | flops | bytes accessed | tf_op | source)
XLA Modules:
  0.0 112.8 jit_solution(12714188035289057958)
XLA Ops:
  0.0 111.0 %experts.1 = bf16[2,48,2048]{2,1,0:T(8,128)(2,1)} custom-call(s32[2,8,48]{2,1,0:T(8,128)} %bitcast.3, s32[2,8,48]{2,1,0:T(8,128)} %bitcast.4, f32[2,8,48]{2,1,0:T(8,128)} %bitcast.5, bf16[2,48,2048]{2,1,0:T(8,128)(2,1)} %tokens_ref.1, bf16[1,2048,1024]{2,1,0:T(8,128)(2,1)} %gate_ref.1, bf16[1,2048,1024]{2,1,0:T(8,128)(2,1)} %up_ref.1, ...), custom_call_target="tpu_custom_call" | custom-call | flops 12884901888 | bytes 12582912 | tf_op jit(solution)/shard_map/experts/pallas_call | solution.py:286
  111.0 1.8 %copy.9 = bf16[2,48,2048]{2,1,0:T(8,128)(2,1)} copy(bf16[2,48,2048]{2,1,0:T(8,128)(2,1)} %experts.1) | data formatting | bytes 786432

commit v3 on v2

v3 whole, which is shorter than its diff:
```python
import jax
import jax.numpy as jnp
from jax import lax
from jax.experimental import pallas as pl
from jax.experimental.pallas import tpu as pltpu
from jax.sharding import PartitionSpec as P

MESH = pl.DeviceIdType.MESH
RING = 8
FAR = RING // 2
GROUP = 8
SLOTS = 8
ROWS = 2 * SLOTS
STAGE = GROUP * ROWS
UP, DOWN = 0, 1

STAGES = 8
STEPS = (0, 1, 7, 2, 6, 3, 5, 4)
FIRST = 5
EARLY = (3,)
LATE = (7, 5, 6, 4, 1, 2, 0)
SIDE = 256
ACROSS = GROUP // 2


def stage_of(d, way):
    return 0 if d == 0 else STAGES - 1 if d == FAR else 2 * d - 1 + way


def kernel(
    ids_ref, places_ref, gates_ref, tokens_ref, gate_ref, up_ref, down_ref, out_ref,
    wg, wu, wd, ids, places, gates, blocks, meta, snd, rcv, hidden, answers, ret, rs_out, rs_in, result,
    side_blocks, side_meta, side_snd, side_ret, side_out, side_in, side_own,
    weight_sem, tok_sem, route_sem, out_sem,
    meta_send, meta_recv, ag_send, ag_recv, d_send, d_recv, r_send, r_recv, rs_send, rs_recv,
    sb_send, sb_recv, sm_send, sm_recv, sd_send, sd_recv, sr_send, sr_recv, sx_send, sx_recv,
):
    micro, tok, width = tokens_ref.shape
    pair = micro * tok
    half = (width - SIDE) // 2
    chunks = [slice(SIDE, SIDE + half), slice(SIDE + half, width)]
    side = slice(0, SIDE)
    ex, ey = lax.axis_index("ex"), lax.axis_index("ey")
    z = ex // 2
    y = lax.rem(ex, 2) * 2 + ey // 2
    core = lax.rem(ey, 2)

    def device(dz, dy, dc):
        there_z = lax.rem(z + dz + RING, RING)
        there_y = lax.rem(y + dy + ACROSS, ACROSS)
        there_core = lax.rem(core + dc, 2)
        return {"ex": there_z * 2 + there_y // 2, "ey": lax.rem(there_y, 2) * 2 + there_core}

    def partner(r, back=False):
        return device(0, -(r // 2) if back else r // 2, r % 2)

    def remote(src, dst, send, recv, there):
        return pltpu.make_async_remote_copy(
            src_ref=src, dst_ref=dst, send_sem=send, recv_sem=recv, device_id=there, device_id_type=MESH
        )

    met = [partner(r) for r in range(1, GROUP)] + [device(1, 0, 0), device(-1, 0, 0)]
    barrier = pltpu.get_barrier_semaphore()
    for there in met:
        pl.semaphore_signal(barrier, inc=1, device_id=there, device_id_type=MESH)

    tok_copies = [
        pltpu.make_async_copy(tokens_ref.at[m], blocks.at[0, pl.ds(m * tok, tok)], tok_sem.at[m])
        for m in range(micro)
    ]
    route_copies = [
        pltpu.make_async_copy(src, dst, route_sem.at[i])
        for i, (src, dst) in enumerate(((ids_ref, ids), (places_ref, places), (gates_ref, gates)))
    ]
    weight_copies = [
        pltpu.make_async_copy(src.at[0], dst, weight_sem.at[i])
        for i, (src, dst) in enumerate(((gate_ref, wg), (up_ref, wu), (down_ref, wd)))
    ]
    for copy in tok_copies + route_copies + weight_copies:
        copy.start()

    meta[0] = jnp.zeros_like(meta[0])
    for copy in route_copies:
        copy.wait()
    for m in range(micro):
        code = jnp.where(places[m] >= 0, ids[m] * SLOTS + places[m], -1)
        meta[0, m, 0:8, 0:tok] = code.astype(jnp.float32)
        meta[0, m, 8:16, 0:tok] = gates[m]
    for copy in tok_copies:
        copy.wait()
    pl.semaphore_wait(barrier, len(met))

    sent = []

    def start(copy):
        copy.start()
        sent.append(copy)

    def block_copy(d, way, m, c):
        at = pl.ds(m * tok, tok)
        return remote(
            blocks.at[stage_of(d, way), at, chunks[c]], blocks.at[stage_of(d + 1, way), at, chunks[c]],
            ag_send.at[way, d, m, c], ag_recv.at[way, d, m, c], device(1 if way == UP else -1, 0, 0),
        )

    def meta_copy(d, way):
        return remote(
            meta.at[stage_of(d, way)], meta.at[stage_of(d + 1, way)],
            meta_send.at[way, d], meta_recv.at[way, d], device(1 if way == UP else -1, 0, 0),
        )

    def pass_block(d, way, m, c):
        if d < FAR - 1 or c == way:
            start(block_copy(d, way, m, c))

    def pass_meta(d, way):
        if d < FAR - 1 or way == UP:
            start(meta_copy(d, way))

    lane = lax.broadcasted_iota(jnp.int32, (8, 128), 1)

    def joined(both):
        return jnp.where(lane < tok, both[0], pltpu.roll(both[1], tok, 1))

    def cells(info, mode):
        found = []
        for m in range(micro):
            code = info[m, 0:8, :].astype(jnp.int32)
            expert = code // SLOTS
            far, near = expert // GROUP, lax.rem(expert, GROUP)
            turn = lax.rem(near // 2 - y + ACROSS, ACROSS)
            other = lax.rem(near + core, 2)
            if mode == "side":
                u = lax.rem(far - z + RING, RING)
                stage = jnp.where(u == 0, 0, jnp.where(u < FAR, 2 * u - 1, jnp.where(u == FAR, 7, 2 * (RING - u))))
                good = turn == 0
                at = stage * 2 + other
            else:
                good = far == z
                at = turn * 2 + other
            at = at * ROWS + m * SLOTS + lax.rem(code, SLOTS)
            found.append(jnp.where((code >= 0) & good & (lane < tok), at, -1))
        return joined(found)

    def select(info, mode, rows):
        where = cells(info, mode)
        row = lax.broadcasted_iota(jnp.int32, (rows, 128), 0)
        hit = row == where[0:1, :]
        for k in range(1, 8):
            hit = hit | (row == where[k : k + 1, :])
        return jnp.where(hit, 1.0, 0.0).astype(jnp.bfloat16)[:, 0:pair]

    def mixing(info, mode, rows):
        where = cells(info, mode)
        weight = joined([info[m, 8:16, :] for m in range(micro)])
        row = lax.broadcasted_iota(jnp.int32, (rows, 128), 0)
        total = jnp.zeros((rows, 128), jnp.float32)
        for k in range(8):
            total = total + jnp.where(row == where[k : k + 1, :], weight[k : k + 1, :], 0.0)
        total = total.T[0:pair]
        high = total.astype(jnp.bfloat16)
        low = (total - high.astype(jnp.float32)).astype(jnp.bfloat16)
        return high, low

    def mix(weights, rows):
        high, low = weights
        return jnp.dot(high, rows, preferred_element_type=jnp.float32) + jnp.dot(
            low, rows, preferred_element_type=jnp.float32
        )

    def rows_of(stage, r):
        return pl.ds(stage * STAGE + r * ROWS, ROWS)

    def all_rows(stage):
        return pl.ds(stage * STAGE + ROWS, STAGE - ROWS)

    def dispatched(stage, c):
        there = snd.at[all_rows(stage), chunks[c]]
        return remote(there, there, d_send.at[stage, c], d_recv.at[stage, c], device(0, 0, 0))

    def returned(stage, c):
        there = ret.at[all_rows(stage), chunks[c]]
        return remote(there, there, r_send.at[stage, c], r_recv.at[stage, c], device(0, 0, 0))

    def side_dispatch(stage, q):
        return remote(
            side_snd.at[stage, q], rcv.at[stage, :, q, :, side],
            sd_send.at[stage, q], sd_recv.at[stage, q], device(STEPS[stage], 0, q),
        )

    def side_return(stage, q):
        return remote(
            answers.at[stage, :, q, :, side], side_ret.at[stage, q],
            sr_send.at[stage, q], sr_recv.at[stage, q], device(-STEPS[stage], 0, q),
        )

    side_block_copies, side_meta_copies = {}, {}
    for t in range(1, ACROSS):
        side_block_copies[t] = remote(
            blocks.at[0, :, side], side_blocks.at[t], sb_send.at[t], sb_recv.at[t], device(0, t, 0)
        )
        side_meta_copies[t] = remote(meta.at[0], side_meta.at[t], sm_send.at[t], sm_recv.at[t], device(0, t, 0))

    def side_info(t):
        return side_meta.at[t] if t else meta.at[0]

    for way in (UP, DOWN):
        pass_block(0, way, 0, 0)
        pass_meta(0, way)
    for m, c in ((1, 0), (0, 1), (1, 1)):
        for way in (UP, DOWN):
            pass_block(0, way, m, c)
    for t in (1, 3, 2):
        start(side_meta_copies[t])
        start(side_block_copies[t])

    def dispatch(stage, c, choice):
        chosen = jnp.dot(
            choice, blocks[stage, :, chunks[c]], preferred_element_type=jnp.float32
        ).astype(jnp.bfloat16)
        base = stage * STAGE
        rcv[stage, 0, 0, :, chunks[c]] = chosen[0:ROWS]
        snd[base + ROWS : base + STAGE, chunks[c]] = chosen[ROWS:STAGE]
        for r in range(1, GROUP):
            remote(
                snd.at[rows_of(stage, r), chunks[c]], rcv.at[stage, r // 2, r % 2, :, chunks[c]],
                d_send.at[stage, c], d_recv.at[stage, c], partner(r),
            ).start()

    def choose_side():
        for t in (0, 1, 3, 2):
            if t:
                side_meta_copies[t].wait_recv()
                side_block_copies[t].wait_recv()
            choice = select(side_info(t), "side", 2 * STAGE)
            tokens = side_blocks[t] if t else blocks[0, :, side]
            chosen = jnp.dot(choice, tokens, preferred_element_type=jnp.float32).astype(jnp.bfloat16)
            side_snd[:, :, t] = chosen.reshape(STAGES, 2, ROWS, SIDE)
        rcv[0, :, 0, :, side] = side_snd[0, 0]

    def dispatch_side(*stages):
        for stage in stages:
            for q in range(2):
                if (stage, q) != (0, 0):
                    start(side_dispatch(stage, q))

    def ways(d):
        return (UP, DOWN) if 0 < d < FAR else (UP,)

    def dispatch_step(d):
        choices = {}
        for c in range(2):
            for m in range(micro):
                for way in ways(d):
                    if d == FAR:
                        block_copy(d - 1, c, m, c).wait_recv()
                    elif d:
                        block_copy(d - 1, way, m, c).wait_recv()
                        pass_block(d, way, m, c)
                    if d and (m, c) == (0, 0):
                        meta_copy(d - 1, way).wait_recv()
                        if d < FAR:
                            pass_meta(d, way)
            for way in ways(d):
                stage = stage_of(d, way)
                if c == 0:
                    choices[way] = select(meta.at[stage], "ring", STAGE)
                dispatch(stage, c, choices[way])

    tile = 256

    def await_rows(first, last):
        for stage in range(first, last):
            for c in range(2):
                dispatched(stage, c).wait_recv()
            for q in range(2):
                if (stage, q) != (0, 0):
                    side_dispatch(stage, q).wait_recv()

    def expert_up(first, last):
        @pl.loop(0, wg.shape[1] // tile)
        def _(i):
            at = pl.ds(pl.multiple_of(i * tile, tile), tile)
            rows = rcv[first:last].reshape((last - first) * STAGE, width)
            gate_part = jnp.dot(rows, wg[:, at], preferred_element_type=jnp.float32)
            up_part = jnp.dot(rows, wu[:, at], preferred_element_type=jnp.float32)
            hidden[first * STAGE : last * STAGE, at] = (
                gate_part / (1.0 + jnp.exp(-gate_part)) * up_part
            ).astype(jnp.bfloat16)

    def expert_down(first, last):
        @pl.loop(0, width // tile)
        def _(i):
            at = pl.ds(pl.multiple_of(i * tile, tile), tile)
            answer = jnp.dot(
                hidden[first * STAGE : last * STAGE], wd[:, at], preferred_element_type=jnp.float32
            )
            answers[first:last, :, :, :, at] = answer.astype(jnp.bfloat16).reshape(
                last - first, ACROSS, 2, ROWS, tile
            )

    def give_back(stage):
        for c in range(2):
            for r in range(1, GROUP):
                remote(
                    answers.at[stage, r // 2, r % 2, :, chunks[c]], ret.at[rows_of(stage, r), chunks[c]],
                    r_send.at[stage, c], r_recv.at[stage, c], partner(r, True),
                ).start()
        ret[stage * STAGE : stage * STAGE + ROWS, :] = answers[stage, 0, 0]

    def give_back_side(stage):
        for q in range(2):
            if (stage, q) == (0, 0):
                side_ret[0, 0] = answers[0, :, 0, :, side]
            else:
                start(side_return(stage, q))

    dispatch_step(0)
    dispatch_step(1)
    dispatch_step(2)
    choose_side()
    dispatch_side(1, 2, 3, 4, 0)
    dispatch_step(3)
    dispatch_side(5, 6)
    for copy in weight_copies:
        copy.wait()
    await_rows(0, FIRST)
    expert_up(0, FIRST)
    dispatch_step(FAR)
    dispatch_side(7)
    expert_down(0, FIRST)
    for stage in EARLY:
        give_back(stage)
    for stage in range(FIRST):
        give_back_side(stage)
    await_rows(FIRST, STAGES)
    expert_up(FIRST, STAGES)
    expert_down(FIRST, STAGES)
    for stage in LATE:
        give_back(stage)
        if stage == STAGES - 1:
            for other in range(FIRST, STAGES):
                give_back_side(other)

    def sum_copy(d, way, m, c):
        at = pl.ds(m * tok, tok)
        return remote(
            rs_out.at[way, d - 1, at, chunks[c]], rs_in.at[way, d - 1, at, chunks[c]],
            rs_send.at[way, d - 1, m, c], rs_recv.at[way, d - 1, m, c], device(-1 if way == UP else 1, 0, 0),
        )

    def send_sum(d, way, m, c, value):
        rs_out[way, d - 1, m * tok : (m + 1) * tok, chunks[c]] = value.astype(jnp.bfloat16)
        start(sum_copy(d, way, m, c))

    def side_sum(t):
        return remote(side_out.at[t], side_in.at[t], sx_send.at[t], sx_recv.at[t], device(0, -t, 0))

    def combine_side():
        for stage in range(STAGES):
            for q in range(2):
                if (stage, q) != (0, 0):
                    side_return(stage, q).wait_recv()
        for t in (2, 1, 3, 0):
            part = mix(mixing(side_info(t), "side", 2 * STAGE), side_ret[:, :, t].reshape(2 * STAGE, SIDE))
            if t:
                side_out[t] = part.astype(jnp.bfloat16)
                start(side_sum(t))
            else:
                side_own[...] = part

    for d in reversed(range(FAR + 1)):
        weights = {way: mixing(meta.at[stage_of(d, way)], "ring", STAGE) for way in ways(d)}
        for c in range(2):
            parts = {}
            for way in ways(d):
                stage = stage_of(d, way)
                returned(stage, c).wait_recv()
                parts[way] = mix(weights[way], ret[stage * STAGE : (stage + 1) * STAGE, chunks[c]])
            for m in range(micro):
                at = slice(m * tok, (m + 1) * tok)
                for way in ways(d):
                    mine = parts[way][at]
                    if d == FAR:
                        send_sum(d, c, m, c, mine)
                    elif d:
                        if d < FAR - 1 or c == way:
                            sum_copy(d + 1, way, m, c).wait_recv()
                            mine = mine + rs_in[way, d, at, chunks[c]].astype(jnp.float32)
                        send_sum(d, way, m, c, mine)
                    else:
                        for come in (UP, DOWN):
                            sum_copy(1, come, m, c).wait_recv()
                            mine = mine + rs_in[come, 0, at, chunks[c]].astype(jnp.float32)
                        result[m, :, chunks[c]] = mine.astype(jnp.bfloat16)
        if d == FAR - 1:
            combine_side()
        if d == 1:
            total = side_own[...]
            for t in range(1, ACROSS):
                side_sum(t).wait_recv()
                total = total + side_in[t].astype(jnp.float32)
            for m in range(micro):
                result[m, :, side] = total[m * tok : (m + 1) * tok].astype(jnp.bfloat16)
    out_copy = pltpu.make_async_copy(result, out_ref, out_sem)
    out_copy.start()

    for copy in sent:
        copy.wait_send()
    for stage in range(STAGES):
        for c in range(2):
            dispatched(stage, c).wait_send()
            returned(stage, c).wait_send()
    out_copy.wait()


def per_device(tokens, expert_ids, slot_ids, gate_values, gate_weight, up_weight, down_weight):
    micro, tok, width = tokens.shape
    hid = gate_weight.shape[2]
    bf16, f32, i32 = jnp.bfloat16, jnp.float32, jnp.int32
    anywhere = pl.BlockSpec(memory_space=pl.ANY)
    dma = pltpu.SemaphoreType.DMA
    slots, pair = STAGES * STAGE, micro * tok
    routes = [a.swapaxes(1, 2) for a in (expert_ids, slot_ids, gate_values)]
    return pl.pallas_call(
        kernel,
        out_shape=jax.ShapeDtypeStruct((micro, tok, width), bf16),
        in_specs=[anywhere] * 7,
        out_specs=anywhere,
        scratch_shapes=[
            pltpu.VMEM((width, hid), bf16),
            pltpu.VMEM((width, hid), bf16),
            pltpu.VMEM((hid, width), bf16),
            pltpu.VMEM((micro, 8, tok), i32),
            pltpu.VMEM((micro, 8, tok), i32),
            pltpu.VMEM((micro, 8, tok), f32),
            pltpu.VMEM((STAGES, pair, width), bf16),
            pltpu.VMEM((STAGES, micro, 16, 128), f32),
            pltpu.VMEM((slots, width), bf16),
            pltpu.VMEM((STAGES, ACROSS, 2, ROWS, width), bf16),
            pltpu.VMEM((slots, hid), bf16),
            pltpu.VMEM((STAGES, ACROSS, 2, ROWS, width), bf16),
            pltpu.VMEM((slots, width), bf16),
            pltpu.VMEM((2, FAR, pair, width), bf16),
            pltpu.VMEM((2, FAR, pair, width), bf16),
            pltpu.VMEM((micro, tok, width), bf16),
            pltpu.VMEM((ACROSS, pair, SIDE), bf16),
            pltpu.VMEM((ACROSS, micro, 16, 128), f32),
            pltpu.VMEM((STAGES, 2, ACROSS, ROWS, SIDE), bf16),
            pltpu.VMEM((STAGES, 2, ACROSS, ROWS, SIDE), bf16),
            pltpu.VMEM((ACROSS, pair, SIDE), bf16),
            pltpu.VMEM((ACROSS, pair, SIDE), bf16),
            pltpu.VMEM((pair, SIDE), f32),
            dma((3,)),
            dma((micro,)),
            dma((3,)),
            dma,
        ]
        + [dma((2, FAR))] * 2
        + [dma((2, FAR, micro, 2))] * 2
        + [dma((STAGES, 2))] * 4
        + [dma((2, FAR, micro, 2))] * 2
        + [dma((ACROSS,))] * 4
        + [dma((STAGES, 2))] * 4
        + [dma((ACROSS,))] * 2,
        compiler_params=pltpu.CompilerParams(
            collective_id=0, has_side_effects=True, vmem_limit_bytes=60 * 1024 * 1024
        ),
        cost_estimate=pl.CostEstimate(
            flops=2 * slots * 3 * width * hid,
            bytes_accessed=3 * width * hid * 2,
            transcendentals=slots * hid,
        ),
        name="experts",
    )(*routes, tokens, gate_weight, up_weight, down_weight)


def solution(mesh):
    tokens = P(None, ("dp", "ex", "ey"), None)
    weights = P(("ex", "ey"), None, None)
    return jax.shard_map(
        per_device,
        mesh=mesh,
        in_specs=(tokens,) * 4 + (weights,) * 3,
        out_specs=tokens,
        check_vma=False,
    )
```

time: 114 us -> 107 us (0.939)
  Pallas kernels: 111 us -> 104 us
    pallas_call x1, Pallas kernels: 111 us -> 104 us  [per_device(): pl.pallas_call(kernel, out_shape=jax.ShapeDtypeStruct((micro, tok, width)...]
where the time goes in v3:
time: 107 us; the launch traced here: 106 us
  Pallas kernels  104 us (97%)
  local copies, waits for them, and re-layouts  1.77 us (2%)
    pallas_call x1, Pallas kernels, per_device(): pl.pallas_call(kernel, out_shape=jax.ShapeDtypeStruct((micro, tok, width)...  104 us

profile of v3, /device:TPU:6, one launch (start us, length us, event | category | flops | bytes accessed | tf_op | source)
XLA Modules:
  0.0 105.5 jit_solution(8552892257856292584)
XLA Ops:
  0.0 103.8 %experts.1 = bf16[2,48,2048]{2,1,0:T(8,128)(2,1)} custom-call(s32[2,8,48]{2,1,0:T(8,128)} %bitcast.3, s32[2,8,48]{2,1,0:T(8,128)} %bitcast.4, f32[2,8,48]{2,1,0:T(8,128)} %bitcast.5, bf16[2,48,2048]{2,1,0:T(8,128)(2,1)} %tokens_ref.1, bf16[1,2048,1024]{2,1,0:T(8,128)(2,1)} %gate_ref.1, bf16[1,2048,1024]{2,1,0:T(8,128)(2,1)} %up_ref.1, ...), custom_call_target="tpu_custom_call" | custom-call | flops 12884901888 | bytes 12582912 | tf_op jit(solution)/shard_map/experts/pallas_call | solution.py:425
  103.8 1.8 %copy.9 = bf16[2,48,2048]{2,1,0:T(8,128)(2,1)} copy(bf16[2,48,2048]{2,1,0:T(8,128)(2,1)} %experts.1) | data formatting | bytes 786432

commit v4 on v3

--- a/solution.py
+++ b/solution.py
@@ -18,7 +18,6 @@
 STEPS = (0, 1, 7, 2, 6, 3, 5, 4)
 FIRST = 5
 EARLY = (3,)
-LATE = (7, 5, 6, 4, 1, 2, 0)
 SIDE = 256
 ACROSS = GROUP // 2
 
@@ -29,7 +28,7 @@
 
 def kernel(
     ids_ref, places_ref, gates_ref, tokens_ref, gate_ref, up_ref, down_ref, out_ref,
-    wg, wu, wd, ids, places, gates, blocks, meta, snd, rcv, hidden, answers, ret, rs_out, rs_in, result,
+    wg, wu, wd, ids, places, gates, blocks, meta, spare, snd, rcv, hidden, answers, ret, rs_out, rs_in, result,
     side_blocks, side_meta, side_snd, side_ret, side_out, side_in, side_own,
     weight_sem, tok_sem, route_sem, out_sem,
     meta_send, meta_recv, ag_send, ag_recv, d_send, d_recv, r_send, r_recv, rs_send, rs_recv,
@@ -37,8 +36,8 @@
 ):
     micro, tok, width = tokens_ref.shape
     pair = micro * tok
-    half = (width - SIDE) // 2
-    chunks = [slice(SIDE, SIDE + half), slice(SIDE + half, width)]
+    middle = SIDE + (width - SIDE + 128) // 256 * 128
+    chunks = [slice(SIDE, middle), slice(middle, width)]
     side = slice(0, SIDE)
     ex, ey = lax.axis_index("ex"), lax.axis_index("ey")
     z = ex // 2
@@ -79,16 +78,18 @@
     for copy in tok_copies + route_copies + weight_copies:
         copy.start()
 
-    meta[0] = jnp.zeros_like(meta[0])
+    lane = lax.broadcasted_iota(jnp.int32, (8, 128), 1)
+    spare[...] = jnp.zeros_like(spare)
     for copy in route_copies:
         copy.wait()
     for m in range(micro):
         code = jnp.where(places[m] >= 0, ids[m] * SLOTS + places[m], -1)
-        meta[0, m, 0:8, 0:tok] = code.astype(jnp.float32)
-        meta[0, m, 8:16, 0:tok] = gates[m]
+        spare[m, 0:8, 0:tok] = code.astype(jnp.float32)
+        spare[m, 8:16, 0:tok] = gates[m]
+    for rows in (slice(0, 8), slice(8, 16)):
+        meta[0, rows] = jnp.where(lane < tok, spare[0, rows], pltpu.roll(spare[1, rows], tok, 1))
     for copy in tok_copies:
         copy.wait()
-    pl.semaphore_wait(barrier, len(met))
 
     sent = []
 
@@ -100,13 +101,13 @@
         at = pl.ds(m * tok, tok)
         return remote(
             blocks.at[stage_of(d, way), at, chunks[c]], blocks.at[stage_of(d + 1, way), at, chunks[c]],
-            ag_send.at[way, d, m, c], ag_recv.at[way, d, m, c], device(1 if way == UP else -1, 0, 0),
+            ag_send.at[way, d, m, c], ag_recv.at[way, d, m, c], device(1 - 2 * way, 0, 0),
         )
 
     def meta_copy(d, way):
         return remote(
             meta.at[stage_of(d, way)], meta.at[stage_of(d + 1, way)],
-            meta_send.at[way, d], meta_recv.at[way, d], device(1 if way == UP else -1, 0, 0),
+            meta_send.at[way, d], meta_recv.at[way, d], device(1 - 2 * way, 0, 0),
         )
 
     def pass_block(d, way, m, c):
@@ -117,30 +118,22 @@
         if d < FAR - 1 or way == UP:
             start(meta_copy(d, way))
 
-    lane = lax.broadcasted_iota(jnp.int32, (8, 128), 1)
-
-    def joined(both):
-        return jnp.where(lane < tok, both[0], pltpu.roll(both[1], tok, 1))
-
     def cells(info, mode):
-        found = []
-        for m in range(micro):
-            code = info[m, 0:8, :].astype(jnp.int32)
-            expert = code // SLOTS
-            far, near = expert // GROUP, lax.rem(expert, GROUP)
-            turn = lax.rem(near // 2 - y + ACROSS, ACROSS)
-            other = lax.rem(near + core, 2)
-            if mode == "side":
-                u = lax.rem(far - z + RING, RING)
-                stage = jnp.where(u == 0, 0, jnp.where(u < FAR, 2 * u - 1, jnp.where(u == FAR, 7, 2 * (RING - u))))
-                good = turn == 0
-                at = stage * 2 + other
-            else:
-                good = far == z
-                at = turn * 2 + other
-            at = at * ROWS + m * SLOTS + lax.rem(code, SLOTS)
-            found.append(jnp.where((code >= 0) & good & (lane < tok), at, -1))
-        return joined(found)
+        code = info[0:8, :].astype(jnp.int32)
+        expert = code // SLOTS
+        far, near = expert // GROUP, lax.rem(expert, GROUP)
+        turn = lax.rem(near // 2 - y + ACROSS, ACROSS)
+        other = lax.rem(near + core, 2)
+        if mode == "side":
+            u = lax.rem(far - z + RING, RING)
+            stage = jnp.where(u == 0, 0, jnp.where(u < FAR, 2 * u - 1, jnp.where(u == FAR, 7, 2 * (RING - u))))
+            good = turn == 0
+            at = stage * 2 + other
+        else:
+            good = far == z
+            at = turn * 2 + other
+        at = at * ROWS + jnp.where(lane < tok, 0, SLOTS) + lax.rem(code, SLOTS)
+        return jnp.where((code >= 0) & good & (lane < pair), at, -1)
 
     def select(info, mode, rows):
         where = cells(info, mode)
@@ -152,7 +145,7 @@
 
     def mixing(info, mode, rows):
         where = cells(info, mode)
-        weight = joined([info[m, 8:16, :] for m in range(micro)])
+        weight = info[8:16, :]
         row = lax.broadcasted_iota(jnp.int32, (rows, 128), 0)
         total = jnp.zeros((rows, 128), jnp.float32)
         for k in range(8):
@@ -168,11 +161,15 @@
             low, rows, preferred_element_type=jnp.float32
         )
 
-    def rows_of(stage, r):
-        return pl.ds(stage * STAGE + r * ROWS, ROWS)
+    def rows_of(stage, r, count=1):
+        at = stage * STAGE + r * ROWS
+        return pl.ds(at if isinstance(at, int) else pl.multiple_of(at, ROWS), count * ROWS)
 
     def all_rows(stage):
-        return pl.ds(stage * STAGE + ROWS, STAGE - ROWS)
+        return rows_of(stage, 1, GROUP - 1)
+
+    soon = jnp.where(lax.rem(z, FAR) == 0, DOWN, UP)
+    slow = jnp.where(lax.rem(z, FAR) == FAR - 1, DOWN, UP)
 
     def dispatched(stage, c):
         there = snd.at[all_rows(stage), chunks[c]]
@@ -204,28 +201,35 @@
     def side_info(t):
         return side_meta.at[t] if t else meta.at[0]
 
-    for way in (UP, DOWN):
-        pass_block(0, way, 0, 0)
-        pass_meta(0, way)
-    for m, c in ((1, 0), (0, 1), (1, 1)):
-        for way in (UP, DOWN):
-            pass_block(0, way, m, c)
-    for t in (1, 3, 2):
-        start(side_meta_copies[t])
-        start(side_block_copies[t])
-
-    def dispatch(stage, c, choice):
+    def choose(stage, c, choice):
         chosen = jnp.dot(
             choice, blocks[stage, :, chunks[c]], preferred_element_type=jnp.float32
         ).astype(jnp.bfloat16)
-        base = stage * STAGE
         rcv[stage, 0, 0, :, chunks[c]] = chosen[0:ROWS]
-        snd[base + ROWS : base + STAGE, chunks[c]] = chosen[ROWS:STAGE]
+        snd[all_rows(stage), chunks[c]] = chosen[ROWS:STAGE]
+
+    def dispatch(stage, c):
         for r in range(1, GROUP):
             remote(
                 snd.at[rows_of(stage, r), chunks[c]], rcv.at[stage, r // 2, r % 2, :, chunks[c]],
                 d_send.at[stage, c], d_recv.at[stage, c], partner(r),
             ).start()
+
+    choice = select(meta.at[0], "ring", STAGE)
+    for c in range(2):
+        choose(0, c, choice)
+    pl.semaphore_wait(barrier, len(met))
+    for way in (UP, DOWN):
+        pass_block(0, way, 0, 0)
+        pass_meta(0, way)
+    for t in (1, 3, 2):
+        start(side_meta_copies[t])
+        start(side_block_copies[t])
+    for m, c in ((1, 0), (0, 1), (1, 1)):
+        for way in (UP, DOWN):
+            pass_block(0, way, m, c)
+    for c in range(2):
+        dispatch(0, c)
 
     def choose_side():
         for t in (0, 1, 3, 2):
@@ -247,27 +251,41 @@
     def ways(d):
         return (UP, DOWN) if 0 < d < FAR else (UP,)
 
+    def take(d, way, m, c):
+        if d == FAR:
+            block_copy(d - 1, c, m, c).wait_recv()
+        else:
+            block_copy(d - 1, way, m, c).wait_recv()
+            pass_block(d, way, m, c)
+        if (m, c) == (0, 0):
+            meta_copy(d - 1, way).wait_recv()
+            if d < FAR:
+                pass_meta(d, way)
+
     def dispatch_step(d):
         choices = {}
+
+        def place(i, way, c):
+            stage = stage_of(d, way)
+            if c == 0:
+                choices[i] = select(meta.at[stage], "ring", STAGE)
+            choose(stage, c, choices[i])
+            dispatch(stage, c)
+
         for c in range(2):
-            for m in range(micro):
-                for way in ways(d):
-                    if d == FAR:
-                        block_copy(d - 1, c, m, c).wait_recv()
-                    elif d:
-                        block_copy(d - 1, way, m, c).wait_recv()
-                        pass_block(d, way, m, c)
-                    if d and (m, c) == (0, 0):
-                        meta_copy(d - 1, way).wait_recv()
-                        if d < FAR:
-                            pass_meta(d, way)
-            for way in ways(d):
-                stage = stage_of(d, way)
-                if c == 0:
-                    choices[way] = select(meta.at[stage], "ring", STAGE)
-                dispatch(stage, c, choices[way])
-
-    tile = 256
+            if d == 1:
+                for i, way in enumerate((soon, 1 - soon)):
+                    for m in range(micro):
+                        take(d, way, m, c)
+                    place(i, way, c)
+            else:
+                for m in range(micro):
+                    for way in ways(d):
+                        take(d, way, m, c)
+                for i, way in enumerate(ways(d)):
+                    place(i, way, c)
+
+    up_tile, down_tile = 512, 1024
 
     def await_rows(first, last):
         for stage in range(first, last):
@@ -278,9 +296,9 @@
                     side_dispatch(stage, q).wait_recv()
 
     def expert_up(first, last):
-        @pl.loop(0, wg.shape[1] // tile)
+        @pl.loop(0, wg.shape[1] // up_tile)
         def _(i):
-            at = pl.ds(pl.multiple_of(i * tile, tile), tile)
+            at = pl.ds(pl.multiple_of(i * up_tile, up_tile), up_tile)
             rows = rcv[first:last].reshape((last - first) * STAGE, width)
             gate_part = jnp.dot(rows, wg[:, at], preferred_element_type=jnp.float32)
             up_part = jnp.dot(rows, wu[:, at], preferred_element_type=jnp.float32)
@@ -289,24 +307,24 @@
             ).astype(jnp.bfloat16)
 
     def expert_down(first, last):
-        @pl.loop(0, width // tile)
+        @pl.loop(0, width // down_tile)
         def _(i):
-            at = pl.ds(pl.multiple_of(i * tile, tile), tile)
+            at = pl.ds(pl.multiple_of(i * down_tile, down_tile), down_tile)
             answer = jnp.dot(
                 hidden[first * STAGE : last * STAGE], wd[:, at], preferred_element_type=jnp.float32
             )
             answers[first:last, :, :, :, at] = answer.astype(jnp.bfloat16).reshape(
-                last - first, ACROSS, 2, ROWS, tile
+                last - first, ACROSS, 2, ROWS, down_tile
             )
 
-    def give_back(stage):
-        for c in range(2):
+    def give_back(stage, parts=(0, 1)):
+        for c in parts:
             for r in range(1, GROUP):
                 remote(
                     answers.at[stage, r // 2, r % 2, :, chunks[c]], ret.at[rows_of(stage, r), chunks[c]],
                     r_send.at[stage, c], r_recv.at[stage, c], partner(r, True),
                 ).start()
-        ret[stage * STAGE : stage * STAGE + ROWS, :] = answers[stage, 0, 0]
+            ret[rows_of(stage, 0), chunks[c]] = answers[stage, 0, 0, :, chunks[c]]
 
     def give_back_side(stage):
         for q in range(2):
@@ -315,7 +333,6 @@
             else:
                 start(side_return(stage, q))
 
-    dispatch_step(0)
     dispatch_step(1)
     dispatch_step(2)
     choose_side()
@@ -336,17 +353,23 @@
     await_rows(FIRST, STAGES)
     expert_up(FIRST, STAGES)
     expert_down(FIRST, STAGES)
-    for stage in LATE:
-        give_back(stage)
-        if stage == STAGES - 1:
-            for other in range(FIRST, STAGES):
-                give_back_side(other)
+    give_back(7)
+    for other in range(FIRST, STAGES):
+        give_back_side(other)
+    for c in range(2):
+        for stage in (5, 6):
+            give_back(stage, (c,))
+    give_back(4)
+    for c in range(2):
+        for way in (slow, 1 - slow):
+            give_back(1 + way, (c,))
+    give_back(0)
 
     def sum_copy(d, way, m, c):
         at = pl.ds(m * tok, tok)
         return remote(
             rs_out.at[way, d - 1, at, chunks[c]], rs_in.at[way, d - 1, at, chunks[c]],
-            rs_send.at[way, d - 1, m, c], rs_recv.at[way, d - 1, m, c], device(-1 if way == UP else 1, 0, 0),
+            rs_send.at[way, d - 1, m, c], rs_recv.at[way, d - 1, m, c], device(2 * way - 1, 0, 0),
         )
 
     def send_sum(d, way, m, c, value):
@@ -370,17 +393,16 @@
                 side_own[...] = part
 
     for d in reversed(range(FAR + 1)):
-        weights = {way: mixing(meta.at[stage_of(d, way)], "ring", STAGE) for way in ways(d)}
+        order = (slow, 1 - slow) if d == 1 else ways(d)
+        weights = [mixing(meta.at[stage_of(d, way)], "ring", STAGE) for way in order]
         for c in range(2):
-            parts = {}
-            for way in ways(d):
+            for i, way in enumerate(order):
                 stage = stage_of(d, way)
                 returned(stage, c).wait_recv()
-                parts[way] = mix(weights[way], ret[stage * STAGE : (stage + 1) * STAGE, chunks[c]])
-            for m in range(micro):
-                at = slice(m * tok, (m + 1) * tok)
-                for way in ways(d):
-                    mine = parts[way][at]
+                part = mix(weights[i], ret[rows_of(stage, 0, GROUP), chunks[c]])
+                for m in range(micro):
+                    at = slice(m * tok, (m + 1) * tok)
+                    mine = part[at]
                     if d == FAR:
                         send_sum(d, c, m, c, mine)
                     elif d:
@@ -393,7 +415,7 @@
                             sum_copy(1, come, m, c).wait_recv()
                             mine = mine + rs_in[come, 0, at, chunks[c]].astype(jnp.float32)
                         result[m, :, chunks[c]] = mine.astype(jnp.bfloat16)
-        if d == FAR - 1:
+        if d == FAR - 2:
             combine_side()
         if d == 1:
             total = side_own[...]
@@ -435,7 +457,8 @@
             pltpu.VMEM((micro, 8, tok), i32),
             pltpu.VMEM((micro, 8, tok), f32),
             pltpu.VMEM((STAGES, pair, width), bf16),
-            pltpu.VMEM((STAGES, micro, 16, 128), f32),
+            pltpu.VMEM((STAGES, 16, 128), f32),
+            pltpu.VMEM((micro, 16, 128), f32),
             pltpu.VMEM((slots, width), bf16),
             pltpu.VMEM((STAGES, ACROSS, 2, ROWS, width), bf16),
             pltpu.VMEM((slots, hid), bf16),
@@ -445,7 +468,7 @@
             pltpu.VMEM((2, FAR, pair, width), bf16),
             pltpu.VMEM((micro, tok, width), bf16),
             pltpu.VMEM((ACROSS, pair, SIDE), bf16),
-            pltpu.VMEM((ACROSS, micro, 16, 128), f32),
+            pltpu.VMEM((ACROSS, 16, 128), f32),
             pltpu.VMEM((STAGES, 2, ACROSS, ROWS, SIDE), bf16),
             pltpu.VMEM((STAGES, 2, ACROSS, ROWS, SIDE), bf16),
             pltpu.VMEM((ACROSS, pair, SIDE), bf16),

time: 107 us -> 104 us (0.972)
  Pallas kernels: 104 us -> 102 us
    pallas_call x1, Pallas kernels: 104 us -> 102 us  [per_device(): pl.pallas_call(kernel, out_shape=jax.ShapeDtypeStruct((micro, tok, width)...]
where the time goes in v4:
time: 104 us; the launch traced here: 103 us
  Pallas kernels  102 us (98%)
  local copies, waits for them, and re-layouts  1.77 us (2%)
    pallas_call x1, Pallas kernels, per_device(): pl.pallas_call(kernel, out_shape=jax.ShapeDtypeStruct((micro, tok, width)...  102 us

profile of v4, /device:TPU:6, one launch (start us, length us, event | category | flops | bytes accessed | tf_op | source)
XLA Modules:
  0.0 103.3 jit_solution(4644817064845834881)
XLA Ops:
  0.0 101.6 %experts.1 = bf16[2,48,2048]{2,1,0:T(8,128)(2,1)} custom-call(s32[2,8,48]{2,1,0:T(8,128)} %bitcast.3, s32[2,8,48]{2,1,0:T(8,128)} %bitcast.4, f32[2,8,48]{2,1,0:T(8,128)} %bitcast.5, bf16[2,48,2048]{2,1,0:T(8,128)(2,1)} %tokens_ref.1, bf16[1,2048,1024]{2,1,0:T(8,128)(2,1)} %gate_ref.1, bf16[1,2048,1024]{2,1,0:T(8,128)(2,1)} %up_ref.1, ...), custom_call_target="tpu_custom_call" | custom-call | flops 12884901888 | bytes 12582912 | tf_op jit(solution)/shard_map/experts/pallas_call | solution.py:447
  101.6 1.8 %copy.9 = bf16[2,48,2048]{2,1,0:T(8,128)(2,1)} copy(bf16[2,48,2048]{2,1,0:T(8,128)(2,1)} %experts.1) | data formatting | bytes 786432

commit v5 on v4

--- a/solution.py
+++ b/solution.py
@@ -350,9 +350,10 @@
         give_back(stage)
     for stage in range(FIRST):
         give_back_side(stage)
-    await_rows(FIRST, STAGES)
-    expert_up(FIRST, STAGES)
-    expert_down(FIRST, STAGES)
+    for first, last in ((FIRST, STAGES - 1), (STAGES - 1, STAGES)):
+        await_rows(first, last)
+        expert_up(first, last)
+        expert_down(first, last)
     give_back(7)
     for other in range(FIRST, STAGES):
         give_back_side(other)

time: 104 us -> 102 us (0.981)
  Pallas kernels: 102 us -> 98.6 us
    pallas_call x1, Pallas kernels: 102 us -> 98.6 us  [per_device(): pl.pallas_call(kernel, out_shape=jax.ShapeDtypeStruct((micro, tok, width)...]
where the time goes in v5:
time: 102 us; the launch traced here: 100 us
  Pallas kernels  98.6 us (97%)
  local copies, waits for them, and re-layouts  1.77 us (2%)
    pallas_call x1, Pallas kernels, per_device(): pl.pallas_call(kernel, out_shape=jax.ShapeDtypeStruct((micro, tok, width)...  98.6 us

profile of v5, /device:TPU:6, one launch (start us, length us, event | category | flops | bytes accessed | tf_op | source)
XLA Modules:
  0.0 100.3 jit_solution(1371948991172846031)
XLA Ops:
  0.0 98.6 %experts.1 = bf16[2,48,2048]{2,1,0:T(8,128)(2,1)} custom-call(s32[2,8,48]{2,1,0:T(8,128)} %bitcast.3, s32[2,8,48]{2,1,0:T(8,128)} %bitcast.4, f32[2,8,48]{2,1,0:T(8,128)} %bitcast.5, bf16[2,48,2048]{2,1,0:T(8,128)(2,1)} %tokens_ref.1, bf16[1,2048,1024]{2,1,0:T(8,128)(2,1)} %gate_ref.1, bf16[1,2048,1024]{2,1,0:T(8,128)(2,1)} %up_ref.1, ...), custom_call_target="tpu_custom_call" | custom-call | flops 12884901888 | bytes 12582912 | tf_op jit(solution)/shard_map/experts/pallas_call | solution.py:448
  98.6 1.8 %copy.9 = bf16[2,48,2048]{2,1,0:T(8,128)(2,1)} copy(bf16[2,48,2048]{2,1,0:T(8,128)(2,1)} %experts.1) | data formatting | bytes 786432

commit v6 on v5

--- a/solution.py
+++ b/solution.py
@@ -341,11 +341,14 @@
     dispatch_side(5, 6)
     for copy in weight_copies:
         copy.wait()
-    await_rows(0, FIRST)
-    expert_up(0, FIRST)
+    await_rows(0, 3)
+    expert_up(0, 3)
+    expert_down(0, 3)
     dispatch_step(FAR)
     dispatch_side(7)
-    expert_down(0, FIRST)
+    await_rows(3, FIRST)
+    expert_up(3, FIRST)
+    expert_down(3, FIRST)
     for stage in EARLY:
         give_back(stage)
     for stage in range(FIRST):

time: 102 us -> 101 us (level); the launches traced: 100 us -> 100 us
  no operation moved by 1% of the time
where the time goes in v6:
time: 101 us; the launch traced here: 100 us
  Pallas kernels  98.6 us (98%)
  local copies, waits for them, and re-layouts  1.77 us (2%)
    pallas_call x1, Pallas kernels, per_device(): pl.pallas_call(kernel, out_shape=jax.ShapeDtypeStruct((micro, tok, width)...  98.6 us

profile of v6, /device:TPU:6, one launch (start us, length us, event | category | flops | bytes accessed | tf_op | source)
XLA Modules:
  0.0 100.4 jit_solution(8531710605497653460)
XLA Ops:
  0.0 98.6 %experts.1 = bf16[2,48,2048]{2,1,0:T(8,128)(2,1)} custom-call(s32[2,8,48]{2,1,0:T(8,128)} %bitcast.3, s32[2,8,48]{2,1,0:T(8,128)} %bitcast.4, f32[2,8,48]{2,1,0:T(8,128)} %bitcast.5, bf16[2,48,2048]{2,1,0:T(8,128)(2,1)} %tokens_ref.1, bf16[1,2048,1024]{2,1,0:T(8,128)(2,1)} %gate_ref.1, bf16[1,2048,1024]{2,1,0:T(8,128)(2,1)} %up_ref.1, ...), custom_call_target="tpu_custom_call" | custom-call | flops 12884901888 | bytes 12582912 | tf_op jit(solution)/shard_map/experts/pallas_call | solution.py:451
  98.7 1.8 %copy.9 = bf16[2,48,2048]{2,1,0:T(8,128)(2,1)} copy(bf16[2,48,2048]{2,1,0:T(8,128)(2,1)} %experts.1) | data formatting | bytes 786432
